TPU v7x, 32 devices: a whole 2x2x4 slice. The times are simulated.
32 devices in a mesh: expert: 4 (over z), tensor: 8 (over y, x, core).
Axes of the slice: x: 2, y: 2, z: 4, core: 2. Of those that a mesh axis runs over, the one named last changes fastest.
Arguments:
- activations: bfloat16 [3072, 512], P('tensor', 'expert'), may hold values from -6 to 6
- cotangent: bfloat16 [3072, 512], P('tensor', 'expert'), may hold values from -4 to 4
- route_ids: int32 [512, 2], P('expert'), may hold values from 0 to 3, all different within a row; in each aligned block of 128 rows (0 to 127, 128 to 255, ...) at most 80 rows name the same one
- gate_probs: float32 [512, 2], P('expert'), may hold values from 0.2 to 0.8
- gate_weight: bfloat16 [4, 3072, 16384], P('expert', None, 'tensor'), may hold values from -0.15625 to 0.15625
- up_weight: bfloat16 [4, 3072, 16384], P('expert', None, 'tensor'), may hold values from -0.15625 to 0.15625
- down_weight: bfloat16 [4, 16384, 3072], P('expert', 'tensor'), may hold values from -0.046875 to 0.046875
Outputs:
- grad_input: bfloat16 [3072, 512], P('tensor', 'expert')
- score_grad: float32 [512, 2], P('expert')
Inputs may be any that keep to these rules, and one draw needn't show every extreme that they name: `route_ids`: each token names 2 different experts. Among the 128 tokens of one index of the expert axis no expert is named more than 80 times, and in every draw some such block names one expert exactly 80 times.
All inputs are finite; a program needn't handle non-finite values.
Results may differ from a plain program's by a relative error of at most 0.008.
Values may be sent and summed in bfloat16 or wider, within the bound.
A program may use at most 128 MiB of HBM per device.

v0:
```python
import jax
import jax.numpy as jnp
from jax import lax
from jax.sharding import PartitionSpec as P

EXTRA_ROWS = 16


def slot_numbers(route_ids, expert_count, capacity):
    token_count = route_ids.shape[0]
    onehot = route_ids[:, :, None] == jnp.arange(expert_count, dtype=jnp.int32)[None, None, :]
    named = jnp.sum(onehot.astype(jnp.float32), axis=1).astype(jnp.bfloat16)
    order = jnp.arange(token_count, dtype=jnp.int32)
    before = (order[None, :] < order[:, None]).astype(jnp.bfloat16)
    earlier = jnp.dot(before, named, preferred_element_type=jnp.float32)
    position = jnp.sum(jnp.where(onehot, earlier[:, None, :], 0.0), axis=2).astype(jnp.int32)
    return route_ids * capacity + position


def swiglu_backward(gate_sum, up_sum, hidden_grad):
    sigma = jax.nn.sigmoid(gate_sum)
    silu_value = gate_sum * sigma
    grad_up = (hidden_grad * silu_value).astype(jnp.bfloat16)
    grad_gate = (hidden_grad * up_sum * sigma * (1.0 + gate_sum * (1.0 - sigma))).astype(
        jnp.bfloat16
    )
    score_rows = jnp.sum(silu_value * up_sum * hidden_grad, axis=1)
    return (grad_gate, grad_up, score_rows)


def body(activations, cotangent, route_ids, gate_probs, gate_weight, up_weight, down_weight):
    expert_count = lax.axis_size("expert")
    tokens_here = route_ids.shape[0]
    capacity = min(tokens_here, 5 * tokens_here // (2 * expert_count))
    slot_total = expert_count * capacity
    destination = slot_numbers(route_ids, expert_count, capacity)
    slot_range = jnp.arange(slot_total, dtype=jnp.int32)
    matches = destination[:, :, None] == slot_range[None, None, :]
    placing = jnp.sum(matches.astype(jnp.float32), axis=1).astype(jnp.bfloat16)
    weighting = jnp.sum(jnp.where(matches, gate_probs[:, :, None], jnp.float32(0.0)), axis=1)
    gate_local = gate_weight[0]
    up_local = up_weight[0]
    down_local = down_weight[0]
    first_dims = (((0,), (0,)), ((), ()))
    down_dims = (((0,), (1,)), ((), ()))
    hidden_dims = (((1,), (1,)), ((), ()))
    features_here = activations.shape[0]
    send_in = jnp.dot(activations, placing, preferred_element_type=jnp.float32).astype(jnp.bfloat16)
    send_grad = jnp.dot(cotangent, placing, preferred_element_type=jnp.float32).astype(jnp.bfloat16)
    recv_in, recv_grad = (
        lax.all_to_all(send_in, "expert", split_axis=1, concat_axis=1, tiled=True),
        lax.all_to_all(send_grad, "expert", split_axis=1, concat_axis=1, tiled=True),
    )
    feature_piece = lax.all_gather(recv_in, "tensor", axis=0, tiled=True)
    grad_piece = lax.all_gather(recv_grad, "tensor", axis=0, tiled=True)
    gate_rows = gate_local
    up_rows = up_local
    gate_sum = lax.dot_general(
        feature_piece, gate_rows, first_dims, preferred_element_type=jnp.float32
    )
    up_sum = lax.dot_general(feature_piece, up_rows, first_dims, preferred_element_type=jnp.float32)
    hidden_grad = lax.dot_general(
        grad_piece, down_local, down_dims, preferred_element_type=jnp.float32
    )
    gate_sum, up_sum, hidden_grad = (gate_sum, up_sum, hidden_grad)
    grad_gate, grad_up, score_rows = swiglu_backward(gate_sum, up_sum, hidden_grad)
    gate_rows = gate_local
    up_rows = up_local
    term = lax.dot_general(gate_rows, grad_gate, hidden_dims, preferred_element_type=jnp.float32)
    term = term + lax.dot_general(up_rows, grad_up, hidden_dims, preferred_element_type=jnp.float32)
    tensor_count = lax.axis_size("tensor")
    score_high = score_rows.astype(jnp.bfloat16)
    score_low = (score_rows - score_high.astype(jnp.float32)).astype(jnp.bfloat16)
    extra = jnp.concatenate(
        [
            score_high[None, :],
            score_low[None, :],
            jnp.zeros((EXTRA_ROWS - 2, slot_total), jnp.bfloat16),
        ],
        axis=0,
    )
    blocks = term.astype(jnp.bfloat16).reshape(tensor_count, features_here, slot_total)
    extra = jnp.broadcast_to(extra[None], (tensor_count, EXTRA_ROWS, slot_total))
    parts = lax.all_to_all(
        jnp.concatenate([blocks, extra], axis=1), "tensor", split_axis=0, concat_axis=0, tiled=True
    ).astype(jnp.float32)
    totals = jnp.sum(parts, axis=0)
    score = (
        totals[features_here : features_here + 1] + totals[features_here + 1 : features_here + 2]
    )
    score_high = score.astype(jnp.bfloat16)
    score_low = (score - score_high.astype(jnp.float32)).astype(jnp.bfloat16)
    summed = jnp.concatenate(
        [
            totals[:features_here].astype(jnp.bfloat16),
            score_high,
            score_low,
            jnp.zeros((EXTRA_ROWS - 2, slot_total), jnp.bfloat16),
        ],
        axis=0,
    )
    back = lax.all_to_all(summed, "expert", split_axis=1, concat_axis=1, tiled=True)
    back = back.astype(jnp.float32)
    back_terms = back[:features_here]
    back_scores = (
        back[features_here : features_here + 1] + back[features_here + 1 : features_here + 2]
    )
    grad_local = jnp.dot(
        back_terms, weighting.T, precision=lax.Precision.HIGHEST, preferred_element_type=jnp.float32
    )
    score_grad = jnp.sum(
        jnp.where(matches, back_scores[0][None, None, :], jnp.float32(0.0)), axis=2
    )
    grad_input = grad_local.astype(jnp.bfloat16)
    return (grad_input, score_grad)


def solution(mesh):
    in_specs = (
        P("tensor", "expert"),
        P("tensor", "expert"),
        P("expert", None),
        P("expert", None),
        P("expert", None, "tensor"),
        P("expert", None, "tensor"),
        P("expert", "tensor", None),
    )
    out_specs = (P("tensor", "expert"), P("expert", None))
    return jax.shard_map(body, mesh=mesh, in_specs=in_specs, out_specs=out_specs, check_vma=False)
```

profile of v0, /device:TPU:0, one launch (start us, length us, event | category | flops | bytes accessed | tf_op | source)
XLA Modules:
  0.0 178.5 jit_solution(15263084820237573660)
XLA Ops:
  7.2 0.0 copy-start
  7.2 0.0 all-gather.5.cloned.1.call-start
  7.2 0.7 convert_reduce_fusion.2
  7.9 0.1 fusion.23
  8.1 0.7 select_reduce_fusion.2
  8.8 0.7 convert_add_fusion
  9.5 0.0 copy-done
  9.5 0.2 convolution_convert_fusion
  9.8 14.7 %all_to_all.38 = bf16[384,4,80]{0,2,1:T(8,128)(2,1)} all-to-all(bf16[384,4,80]{0,2,1:T(8,128)(2,1)S(1)} %bitcast.50), channel_id=1, replica_groups=mesh['expert'=4,'tensor'=8] {'expert'}, dimensions={1} | all-to-all | bytes 491520 | tf_op jit(solution)/shard_map/all_to_all | solution.py:51
  24.5 0.0 all-gather.5.cloned.1.call-update
  24.5 0.0 all-gather.3.cloned.1.call-start
  24.6 1.1 convolution_convert_fusion.1
  25.7 10.7 %all_to_all.39 = bf16[384,4,80]{0,2,1:T(8,128)(2,1)} all-to-all(bf16[384,4,80]{0,2,1:T(8,128)(2,1)S(1)} %bitcast.49), channel_id=1, replica_groups=mesh['expert'=4,'tensor'=8] {'expert'}, dimensions={1} | all-to-all | bytes 491520 | tf_op jit(solution)/shard_map/all_to_all | solution.py:52
  36.5 0.0 all-gather.3.cloned.1.call-update
  36.5 14.9 %all-gather.5.cloned.1.call-done = bf16[3072,320]{0,1:T(8,128)(2,1)} async-done(((bf16[384,320]{0,1:T(8,128)(2,1)}), bf16[3072,320]{0,1:T(8,128)(2,1)}) %all-gather.5.cloned.1.call-update) | async-done | bytes 1966096 | tf_op jit(solution)/shard_map/all_gather | solution.py:54
  51.4 0.0 copy-start.3
  51.4 9.4 %fusion.2 = f32[320,2048]{1,0:T(8,128)S(1)} fusion(bf16[3072,320]{0,1:T(8,128)(2,1)} %all-gather.5.cloned.1.call-done, bf16[1,3072,2048]{2,1,0:T(8,128)(2,1)} %param.11), kind=kOutput, calls=%fused_computation.2 | convolution fusion | flops 4026531840 | bytes 17170432 | tf_op jit(solution)/shard_map/dot_general | solution.py:58
  60.8 0.0 copy-done.3
  60.8 8.8 %fusion.6 = f32[320,2048]{1,0:T(8,128)} fusion(bf16[3072,320]{0,1:T(8,128)(2,1)S(1)} %copy-done.3, bf16[1,3072,2048]{2,1,0:T(8,128)(2,1)} %param.12), kind=kOutput, calls=%fused_computation.6 | convolution fusion | flops 4026531840 | bytes 17170432 | tf_op jit(solution)/shard_map/dot_general | solution.py:61
  69.6 11.3 %all-gather.3.cloned.1.call-done = bf16[3072,320]{0,1:T(8,128)(2,1)} async-done(((bf16[384,320]{0,1:T(8,128)(2,1)}), bf16[3072,320]{0,1:T(8,128)(2,1)}) %all-gather.3.cloned.1.call-update) | async-done | bytes 1966096 | tf_op jit(solution)/shard_map/all_gather | solution.py:55
  80.9 12.0 %multiply_reduce_fusion = (f32[320]{0:T(512)S(1)}, f32[320,2048]{1,0:T(8,128)}) fusion(f32[320,2048]{1,0:T(8,128)} %fusion.6, f32[320,2048]{1,0:T(8,128)S(1)} %fusion.2, bf16[3072,320]{0,1:T(8,128)(2,1)} %all-gather.3.cloned.1.call-done, bf16[1,2048,3072]{2,1,0:T(8,128)(2,1)} %param.13), kind=kOutput, calls=%fused_computation.14 | convolution fusion | flops 4031119104 | bytes 22414592 | tf_op jit(solution)/shard_map/dot_general | solution.py:62
  93.0 12.8 %fusion = f32[320,3072]{1,0:T(8,128)} fusion(bf16[1,3072,2048]{2,1,0:T(8,128)(2,1)} %param.11, f32[320,2048]{1,0:T(8,128)S(1)} %fusion.2, f32[320,2048]{1,0:T(8,128)} %get-tuple-element.7, f32[320,2048]{1,0:T(8,128)} %fusion.6), kind=kOutput, calls=%fused_computation | convolution fusion | flops 4033085440 | bytes 24379392 | tf_op jit(solution)/shard_map/dot_general | solution.py:69
  105.8 12.1 %fusion.16 = bf16[3072,320]{0,1:T(8,128)(2,1)} fusion(f32[320,3072]{1,0:T(8,128)} %fusion, bf16[1,3072,2048]{2,1,0:T(8,128)(2,1)} %param.12, f32[320,2048]{1,0:T(8,128)} %get-tuple-element.7, f32[320,2048]{1,0:T(8,128)S(1)} %fusion.2), kind=kOutput, calls=%fused_computation.13 | convolution fusion | flops 4032430080 | bytes 23724032 | tf_op jit(solution)/shard_map/dot_general | solution.py:70
  117.9 2.9 %copy.40 = bf16[3072,320]{1,0:T(8,128)(2,1)S(1)} copy(bf16[3072,320]{0,1:T(8,128)(2,1)} %fusion.16) | data formatting | bytes 3932160 | tf_op jit(solution)/shard_map/reshape | solution.py:82
  120.9 0.3 pad_maximum_fusion
  121.1 33.0 %all_to_all.40 = bf16[8,400,320]{2,1,0:T(8,128)(2,1)S(1)} all-to-all(bf16[8,400,320]{2,1,0:T(8,128)(2,1)S(1)} %pad_maximum_fusion), channel_id=1, replica_groups=mesh['expert'=4,'tensor'=8] {'tensor'}, dimensions={0} | all-to-all | bytes 4096000 | tf_op jit(solution)/shard_map/all_to_all | solution.py:84
  154.1 0.0 copy-start.1
  154.1 0.4 convert_reduce_fusion
  154.5 0.0 copy-start.2
  154.7 0.2 copy.39
  154.8 14.5 %all_to_all.41 = bf16[400,4,80]{0,2,1:T(8,128)(2,1)S(1)} all-to-all(bf16[400,4,80]{0,2,1:T(8,128)(2,1)S(1)} %bitcast.45), channel_id=1, replica_groups=mesh['expert'=4,'tensor'=8] {'expert'}, dimensions={1} | all-to-all | bytes 512000 | tf_op jit(solution)/shard_map/all_to_all | solution.py:102
  169.3 0.1 convert_element_type.115
  169.4 0.2 fusion.22
  169.6 0.1 broadcast_in_dim.57
  169.7 0.0 copy-done.2
  169.7 0.7 select_reduce_fusion
  170.4 1.2 convolution_convert_fusion.2
  171.6 0.0 copy-done.1
  (10 shorter events, 0.2 us)
Async XLA Ops:
  7.2 2.3 %copy-start = (bf16[384,128]{1,0:T(8,128)(2,1)S(1)}, bf16[384,128]{1,0:T(8,128)(2,1)}, u32[]{:S(2)}) copy-start(bf16[384,128]{1,0:T(8,128)(2,1)} %param.7) | copy-start | bytes 294916
  7.2 44.2 %all-gather.5.cloned.1.call-start = ((), (), s32[]{:S(2)}) async-start(), calls=%async_computation.5 | async-start | bytes 2211840 | tf_op jit(solution)/shard_map/all_gather | solution.py:54
  24.5 56.4 %all-gather.3.cloned.1.call-start = ((), (), s32[]{:S(2)}) async-start(), calls=%async_computation.4 | async-start | bytes 2211840 | tf_op jit(solution)/shard_map/all_gather | solution.py:55
  51.4 9.4 %copy-start.3 = (bf16[3072,320]{0,1:T(8,128)(2,1)S(1)}, bf16[3072,320]{0,1:T(8,128)(2,1)}, u32[]{:S(2)}) copy-start(bf16[3072,320]{0,1:T(8,128)(2,1)} %all-gather.5.cloned.1.call-done) | copy-start | bytes 5898244
  154.1 17.5 %copy-start.1 = (bf16[384,128]{1,0:T(8,128)(2,1)S(1)}, bf16[384,128]{1,0:T(8,128)(2,1)}, u32[]{:S(2)}) copy-start(bf16[384,128]{1,0:T(8,128)(2,1)} %param.7) | copy-start | bytes 294916
  154.5 15.2 %copy-start.2 = (f32[128,2]{0,1:T(2,128)S(1)}, f32[128,2]{0,1:T(2,128)}, u32[]{:S(2)}) copy-start(f32[128,2]{0,1:T(2,128)} %param.10) | copy-start | bytes 3076
Sparse Core Ops, SparseCore 0:
  24.7 26.7 all-gather.4
  53.3 27.6 all-gather.2
where the time goes:
time: 179 us; the launch traced here: 178 us
  blocking collectives  73 us (41%)
  matrix products  57.8 us (32%)
  waiting for transfers between devices  26.3 us (15%)
  between operations  14.2 us (8%)
  other arithmetic  3.87 us (2%)
  local copies, waits for them, and re-layouts  3.26 us (2%)
    all_to_all x1, blocking collectives, body(): lax.all_to_all(jnp.concatenate([blocks, extra], axis=1), 'tensor', split_...  33 us
    all_gather x1, waiting for transfers between devices, body(): feature_piece = lax.all_gather(recv_in, 'tensor', axis=0, tiled=True)  14.9 us
    all_to_all x1, blocking collectives, body(): lax.all_to_all(send_in, 'expert', split_axis=1, concat_axis=1, tiled=True)  14.7 us
    all_to_all x1, blocking collectives, body(): lax.all_to_all(summed, 'expert', split_axis=1, concat_axis=1, tiled=True)  14.5 us
    dot_general x1, matrix products, body(): lax.dot_general(gate_rows, grad_gate, hidden_dims, preferred_element_type...  12.8 us
    dot_general x1, matrix products, body(): lax.dot_general(up_rows, grad_up, hidden_dims, preferred_element_type=jnp...  12.1 us
    dot_general x1, matrix products, body(): lax.dot_general(grad_piece, down_local, down_dims, preferred_element_type...  12 us
    all_gather x1, waiting for transfers between devices, body(): grad_piece = lax.all_gather(recv_grad, 'tensor', axis=0, tiled=True)  11.3 us
  transfers between devices with their start and end apart: 2, of which 2 were waited for; matrix products, arithmetic and copies ran while one was open for 11% of the time, Pallas kernels for 0%

commit v1 on v0

--- a/solution.py
+++ b/solution.py
@@ -1,9 +1,26 @@
+import functools
 import jax
 import jax.numpy as jnp
 from jax import lax
 from jax.sharding import PartitionSpec as P
 
 EXTRA_ROWS = 16
+
+
+def stocks_play(page, ndim_at):
+    n_lanes = lax.axis_size("tensor")
+    base_arr = [None] * n_lanes
+    xs_all = [(ix, (ix + 1) % n_lanes) for ix in range(n_lanes)]
+    base_arr[n_lanes - 1] = page
+    for jj in range(n_lanes - 2, -1, -1):
+        base_arr[jj] = lax.ppermute(base_arr[jj + 1], "tensor", xs_all)
+    main = jnp.concatenate(base_arr, axis=ndim_at)
+    v1 = lax.axis_index("tensor")
+    v_next = (v1 + 1) * page.shape[ndim_at]
+    return jnp.roll(main, shift=v_next, axis=ndim_at)
+
+
+screen_process = functools.partial(stocks_play, ndim_at=0)
 
 
 def slot_numbers(route_ids, expert_count, capacity):
@@ -52,7 +69,7 @@
         lax.all_to_all(send_grad, "expert", split_axis=1, concat_axis=1, tiled=True),
     )
     feature_piece = lax.all_gather(recv_in, "tensor", axis=0, tiled=True)
-    grad_piece = lax.all_gather(recv_grad, "tensor", axis=0, tiled=True)
+    grad_piece = screen_process(recv_grad)
     gate_rows = gate_local
     up_rows = up_local
     gate_sum = lax.dot_general(

time: 179 us -> 207 us (1.16)
  waiting for transfers between devices: 26.3 us -> 56.6 us
  blocking collectives: 73 us -> 47.5 us
  local copies, waits for them, and re-layouts: 3.26 us -> 16.2 us
  starting transfers between devices: 0.08 us -> 9.88 us
    ppermute x0 -> x7, waiting for transfers between devices: none -> 43.2 us  [stocks_play(): base_arr[jj] = lax.ppermute(base_arr[jj + 1], 'tensor', xs_all)]
    all_to_all x2 -> x0, blocking collectives: 25.5 us -> none  [the longest x1 14.7 us: body(): lax.all_to_all(send_in, 'expert', split_axis=1, concat_axis=1, tiled=True)]
    all_gather x1, waiting for transfers between devices: 14.9 us -> 0.01 us  [body(): feature_piece = lax.all_gather(recv_in, 'tensor', axis=0, tiled=True)]
    all_to_all x0 -> x2, waiting for transfers between devices: none -> 13.3 us  [the longest x1 6.75 us: body(): lax.all_to_all(send_grad, 'expert', split_axis=1, concat_axis=1, tiled=True)]
    unnamed x8 -> x27, local copies, waits for them, and re-layouts: 0.03 us -> 12.2 us
    all_gather x1 -> x0, waiting for transfers between devices: 11.3 us -> none  [body(): grad_piece = lax.all_gather(recv_grad, 'tensor', axis=0, tiled=True)]
    all_to_all x0 -> x2, starting transfers between devices: none -> 9.71 us  [the longest x1 6.31 us: body(): lax.all_to_all(send_grad, 'expert', split_axis=1, concat_axis=1, tiled=True)]
  transfers between devices with their start and end apart: 2 -> 10, of which waited for: 2 -> 8; matrix products, arithmetic and copies ran while one was open for 11% -> 7% of each run, Pallas kernels for 0% -> 0%
where the time goes in v1:
time: 207 us
  matrix products  58.3 us (28%)
  waiting for transfers between devices  56.6 us (27%)
  blocking collectives  47.5 us (23%)
  local copies, waits for them, and re-layouts  16.2 us (8%)
  between operations  14.2 us (7%)
  starting transfers between devices  9.88 us (5%)
  other arithmetic  3.9 us (2%)
    ppermute x7, waiting for transfers between devices, stocks_play(): base_arr[jj] = lax.ppermute(base_arr[jj + 1], 'tensor', xs_all)  43.2 us
    all_to_all x1, blocking collectives, body(): lax.all_to_all(jnp.concatenate([blocks, extra], axis=1), 'tensor', split_...  33 us
    all_to_all x1, blocking collectives, body(): lax.all_to_all(summed, 'expert', split_axis=1, concat_axis=1, tiled=True)  14.5 us
    dot_general x1, matrix products, body(): lax.dot_general(gate_rows, grad_gate, hidden_dims, preferred_element_type...  12.8 us
    dot_general x1, matrix products, body(): lax.dot_general(grad_piece, down_local, down_dims, preferred_element_type...  12.3 us
    dot_general x1, matrix products, body(): lax.dot_general(up_rows, grad_up, hidden_dims, preferred_element_type=jnp...  12.3 us
    unnamed x27, local copies, waits for them, and re-layouts  12.2 us
    dot_general x1, matrix products, body(): lax.dot_general(feature_piece, gate_rows, first_dims, preferred_element_t...  9.42 us
  transfers between devices with their start and end apart: 10, of which 8 were waited for; matrix products, arithmetic and copies ran while one was open for 7% of the time, Pallas kernels for 0%

profile of v1, /device:TPU:0, one launch (start us, length us, event | category | flops | bytes accessed | tf_op | source)
XLA Modules:
  0.0 206.6 jit_solution(17757942513348049886)
XLA Ops:
  7.2 0.0 copy-start
  7.2 0.7 convert_reduce_fusion.2
  7.9 0.1 fusion.24
  8.0 0.7 select_reduce_fusion.2
  8.8 0.7 convert_add_fusion
  9.5 0.0 copy-done
  9.5 0.9 convolution_convert_fusion.1
  10.4 6.3 %all-to-all-start = ((bf16[384,4,80]{0,2,1:T(8,128)(2,1)}), bf16[384,4,80]{0,2,1:T(8,128)(2,1)S(1)}, u32[]{:S(2)}, u32[]{:S(2)}) async-start(bf16[384,4,80]{0,2,1:T(8,128)(2,1)} %bitcast.1), calls=%async_computation | async-start | bytes 491520 | tf_op jit(solution)/shard_map/all_to_all | solution.py:69
  16.7 1.8 convolution_convert_fusion
  18.6 6.8 %all-to-all-done = bf16[384,4,80]{0,2,1:T(8,128)(2,1)S(1)} async-done(((bf16[384,4,80]{0,2,1:T(8,128)(2,1)}), bf16[384,4,80]{0,2,1:T(8,128)(2,1)S(1)}, u32[]{:S(2)}, u32[]{:S(2)}) %all-to-all-start) | async-done | bytes 245792 | tf_op jit(solution)/shard_map/all_to_all | solution.py:69
  25.3 3.4 %all-to-all-start.1 = ((bf16[384,4,80]{0,2,1:T(8,128)(2,1)}), bf16[384,4,80]{0,2,1:T(8,128)(2,1)S(1)}, u32[]{:S(2)}, u32[]{:S(2)}) async-start(bf16[384,4,80]{0,2,1:T(8,128)(2,1)} %bitcast.5), calls=%async_computation.1 | async-start | bytes 491520 | tf_op jit(solution)/shard_map/all_to_all | solution.py:68
  28.7 0.0 all-gather.2.cloned.1.call-start
  28.8 0.1 collective-permute-start
  28.8 6.5 %all-to-all-done.1 = bf16[384,4,80]{0,2,1:T(8,128)(2,1)S(1)} async-done(((bf16[384,4,80]{0,2,1:T(8,128)(2,1)}), bf16[384,4,80]{0,2,1:T(8,128)(2,1)S(1)}, u32[]{:S(2)}, u32[]{:S(2)}) %all-to-all-start.1) | async-done | bytes 245792 | tf_op jit(solution)/shard_map/all_to_all | solution.py:68
  35.4 0.7 copy-done.2
  36.1 0.0 all-gather.2.cloned.1.call-update
  36.1 0.0 collective-permute-done
  36.1 0.1 collective-permute-start.1
  36.2 6.5 %collective-permute-done.1 = bf16[384,320]{0,1:T(8,128)(2,1)S(1)} collective-permute-done((bf16[384,320]{0,1:T(8,128)(2,1)S(1)}, bf16[384,320]{0,1:T(8,128)(2,1)S(1)}, u32[]{:S(2)}, u32[]{:S(2)}) %collective-permute-start.1) | collective-permute-done | bytes 245792 | tf_op jit(solution)/shard_map/ppermute | solution.py:16
  42.7 0.0 collective-permute-start.2
  42.7 9.2 %collective-permute-done.2 = bf16[384,320]{0,1:T(8,128)(2,1)S(1)} collective-permute-done((bf16[384,320]{0,1:T(8,128)(2,1)S(1)}, bf16[384,320]{0,1:T(8,128)(2,1)S(1)}, u32[]{:S(2)}, u32[]{:S(2)}) %collective-permute-start.2) | collective-permute-done | bytes 245792 | tf_op jit(solution)/shard_map/ppermute | solution.py:16
  51.8 0.0 collective-permute-start.3
  51.8 6.6 %collective-permute-done.3 = bf16[384,320]{0,1:T(8,128)(2,1)S(1)} collective-permute-done((bf16[384,320]{0,1:T(8,128)(2,1)S(1)}, bf16[384,320]{0,1:T(8,128)(2,1)S(1)}, u32[]{:S(2)}, u32[]{:S(2)}) %collective-permute-start.3) | collective-permute-done | bytes 245792 | tf_op jit(solution)/shard_map/ppermute | solution.py:16
  58.4 0.0 collective-permute-start.4
  58.4 7.9 %collective-permute-done.4 = bf16[384,320]{0,1:T(8,128)(2,1)S(1)} collective-permute-done((bf16[384,320]{0,1:T(8,128)(2,1)S(1)}, bf16[384,320]{0,1:T(8,128)(2,1)S(1)}, u32[]{:S(2)}, u32[]{:S(2)}) %collective-permute-start.4) | collective-permute-done | bytes 245792 | tf_op jit(solution)/shard_map/ppermute | solution.py:16
  66.4 0.0 collective-permute-start.5
  66.4 6.5 %collective-permute-done.5 = bf16[384,320]{0,1:T(8,128)(2,1)S(1)} collective-permute-done((bf16[384,320]{0,1:T(8,128)(2,1)S(1)}, bf16[384,320]{0,1:T(8,128)(2,1)S(1)}, u32[]{:S(2)}, u32[]{:S(2)}) %collective-permute-start.5) | collective-permute-done | bytes 245792 | tf_op jit(solution)/shard_map/ppermute | solution.py:16
  72.9 0.0 collective-permute-start.6
  72.9 6.5 %collective-permute-done.6 = bf16[384,320]{0,1:T(8,128)(2,1)S(1)} collective-permute-done((bf16[384,320]{0,1:T(8,128)(2,1)S(1)}, bf16[384,320]{0,1:T(8,128)(2,1)S(1)}, u32[]{:S(2)}, u32[]{:S(2)}) %collective-permute-start.6) | collective-permute-done | bytes 245792 | tf_op jit(solution)/shard_map/ppermute | solution.py:16
  79.4 0.8 constant_dynamic-update-slice_fusion.15
  80.2 0.8 constant_dynamic-update-slice_fusion.14
  81.0 0.7 constant_dynamic-update-slice_fusion.13
  81.7 0.7 constant_dynamic-update-slice_fusion.12
  82.4 0.8 constant_dynamic-update-slice_fusion.11
  83.2 0.8 constant_dynamic-update-slice_fusion.10
  84.0 0.8 constant_dynamic-update-slice_fusion.9
  84.8 0.8 constant_dynamic-update-slice_fusion.8
  85.6 0.8 constant_dynamic-update-slice_fusion.7
  86.4 0.8 constant_dynamic-update-slice_fusion.6
  87.1 0.8 constant_dynamic-update-slice_fusion.5
  87.9 0.8 constant_dynamic-update-slice_fusion.4
  88.6 0.8 constant_dynamic-update-slice_fusion.3
  89.4 0.8 constant_dynamic-update-slice_fusion.2
  90.2 0.8 constant_dynamic-update-slice_fusion.1
  90.9 0.8 constant_dynamic-update-slice_fusion
  91.7 9.4 %fusion.2 = f32[320,2048]{1,0:T(8,128)S(1)} fusion(bf16[3072,320]{0,1:T(8,128)(2,1)} %all-gather.2.cloned.1.call-done, bf16[1,3072,2048]{2,1,0:T(8,128)(2,1)} %param.11), kind=kOutput, calls=%fused_computation.2 | convolution fusion | flops 4026531840 | bytes 17170432 | tf_op jit(solution)/shard_map/dot_general | solution.py:75
  101.1 0.0 copy-done.4
  101.1 7.4 %fusion.6 = f32[320,2048]{1,0:T(8,128)S(1)} fusion(bf16[3072,320]{0,1:T(8,128)(2,1)S(1)} %copy-done.4, bf16[1,3072,2048]{2,1,0:T(8,128)(2,1)} %param.12), kind=kOutput, calls=%fused_computation.6 | convolution fusion | flops 4026531840 | bytes 17170432 | tf_op jit(solution)/shard_map/dot_general | solution.py:78
  108.5 12.3 %multiply_reduce_fusion = (f32[320]{0:T(512)S(1)}, f32[320,2048]{1,0:T(8,128)}) fusion(f32[320,2048]{1,0:T(8,128)S(1)} %fusion.6, f32[320,2048]{1,0:T(8,128)S(1)} %fusion.2, bf16[1,2048,3072]{2,1,0:T(8,128)(2,1)} %param.13, bf16[6144,320]{0,1:T(8,128)(2,1)} %constant_dynamic-update-slice_fusion, s32[]{:T(128)S(6)} %select_n.27), kind=kOutput, calls=%fused_computation.14 | convolution fusion | flops 4031119104 | bytes 22414596 | tf_op jit(solution)/shard_map/dot_general | solution.py:79
  120.9 0.0 copy-done.5
  120.9 12.8 %fusion = f32[320,3072]{1,0:T(8,128)} fusion(bf16[1,3072,2048]{2,1,0:T(8,128)(2,1)} %param.11, f32[320,2048]{1,0:T(8,128)S(1)} %fusion.2, f32[320,2048]{1,0:T(8,128)} %get-tuple-element.7, f32[320,2048]{1,0:T(8,128)} %copy-done.5), kind=kOutput, calls=%fused_computation | convolution fusion | flops 4033085440 | bytes 24379392 | tf_op jit(solution)/shard_map/dot_general | solution.py:86
  133.7 12.3 %fusion.16 = bf16[3072,320]{0,1:T(8,128)(2,1)} fusion(f32[320,3072]{1,0:T(8,128)} %fusion, bf16[1,3072,2048]{2,1,0:T(8,128)(2,1)} %param.12, f32[320,2048]{1,0:T(8,128)} %get-tuple-element.7, f32[320,2048]{1,0:T(8,128)S(1)} %fusion.2), kind=kOutput, calls=%fused_computation.13 | convolution fusion | flops 4032430080 | bytes 23724032 | tf_op jit(solution)/shard_map/dot_general | solution.py:87
  146.0 2.9 %copy.40 = bf16[3072,320]{1,0:T(8,128)(2,1)S(1)} copy(bf16[3072,320]{0,1:T(8,128)(2,1)} %fusion.16) | data formatting | bytes 3932160 | tf_op jit(solution)/shard_map/reshape | solution.py:99
  149.0 0.3 pad_maximum_fusion
  149.3 0.0 copy-start.1
  149.3 33.0 %all_to_all.38 = bf16[8,400,320]{2,1,0:T(8,128)(2,1)S(1)} all-to-all(bf16[8,400,320]{2,1,0:T(8,128)(2,1)S(1)} %pad_maximum_fusion), channel_id=1, replica_groups=mesh['expert'=4,'tensor'=8] {'tensor'}, dimensions={0} | all-to-all | bytes 4096000 | tf_op jit(solution)/shard_map/all_to_all | solution.py:101
  182.3 0.4 convert_reduce_fusion
  182.8 0.2 copy.39
  183.0 14.5 %all_to_all.39 = bf16[400,4,80]{0,2,1:T(8,128)(2,1)S(1)} all-to-all(bf16[400,4,80]{0,2,1:T(8,128)(2,1)S(1)} %bitcast.47), channel_id=1, replica_groups=mesh['expert'=4,'tensor'=8] {'expert'}, dimensions={1} | all-to-all | bytes 512000 | tf_op jit(solution)/shard_map/all_to_all | solution.py:119
  197.5 0.1 convert_element_type.115
  197.5 0.2 fusion.23
  197.8 0.1 broadcast_in_dim.57
  197.9 0.7 select_reduce_fusion
  198.6 1.2 convolution_convert_fusion.2
  (17 shorter events, 0.2 us)
Async XLA Ops:
  7.2 2.3 %copy-start = (bf16[384,128]{1,0:T(8,128)(2,1)S(1)}, bf16[384,128]{1,0:T(8,128)(2,1)}, u32[]{:S(2)}) copy-start(bf16[384,128]{1,0:T(8,128)(2,1)} %param.8) | copy-start | bytes 294916
  10.4 14.9 %all-to-all-start = ((bf16[384,4,80]{0,2,1:T(8,128)(2,1)}), bf16[384,4,80]{0,2,1:T(8,128)(2,1)S(1)}, u32[]{:S(2)}, u32[]{:S(2)}) async-start(bf16[384,4,80]{0,2,1:T(8,128)(2,1)} %bitcast.1), calls=%async_computation | async-start | bytes 491520 | tf_op jit(solution)/shard_map/all_to_all | solution.py:69
  25.3 10.1 %all-to-all-start.1 = ((bf16[384,4,80]{0,2,1:T(8,128)(2,1)}), bf16[384,4,80]{0,2,1:T(8,128)(2,1)S(1)}, u32[]{:S(2)}, u32[]{:S(2)}) async-start(bf16[384,4,80]{0,2,1:T(8,128)(2,1)} %bitcast.5), calls=%async_computation.1 | async-start | bytes 491520 | tf_op jit(solution)/shard_map/all_to_all | solution.py:68
  28.7 63.0 %all-gather.2.cloned.1.call-start = ((), (), s32[]{:S(2)}) async-start(), calls=%async_computation.4 | async-start | bytes 2211840 | tf_op jit(solution)/shard_map/all_gather | solution.py:71
  28.8 7.3 %collective-permute-start = (bf16[384,320]{0,1:T(8,128)(2,1)S(1)}, bf16[384,320]{0,1:T(8,128)(2,1)S(1)}, u32[]{:S(2)}, u32[]{:S(2)}) collective-permute-start(bf16[384,320]{0,1:T(8,128)(2,1)S(1)} %bitcast.44), channel_id=1, source_target_pairs={{0,1},{1,2},{2,3},{3,4},{4,5},{5,6},{6,7},{7,0},{8,9},{9,10},{10,1... | collective-permute-start | bytes 737288 | tf_op jit(solution)/shard_map/ppermute | solution.py:16
  35.4 0.7 copy-start.2
  36.1 6.6 %collective-permute-start.1 = (bf16[384,320]{0,1:T(8,128)(2,1)S(1)}, bf16[384,320]{0,1:T(8,128)(2,1)S(1)}, u32[]{:S(2)}, u32[]{:S(2)}) collective-permute-start(bf16[384,320]{0,1:T(8,128)(2,1)S(1)} %collective-permute-done), channel_id=1, source_target_pairs={{0,1},{1,2},{2,3},{3,4},{4,5},{5,6},{6,7},{7,0},{8,9},{9,10},{10,1... | collective-permute-start | bytes 737288 | tf_op jit(solution)/shard_map/ppermute | solution.py:16
  42.7 9.2 %collective-permute-start.2 = (bf16[384,320]{0,1:T(8,128)(2,1)S(1)}, bf16[384,320]{0,1:T(8,128)(2,1)S(1)}, u32[]{:S(2)}, u32[]{:S(2)}) collective-permute-start(bf16[384,320]{0,1:T(8,128)(2,1)S(1)} %collective-permute-done.1), channel_id=1, source_target_pairs={{0,1},{1,2},{2,3},{3,4},{4,5},{5,6},{6,7},{7,0},{8,9},{9,10},{10,1... | collective-permute-start | bytes 737288 | tf_op jit(solution)/shard_map/ppermute | solution.py:16
  51.8 6.6 %collective-permute-start.3 = (bf16[384,320]{0,1:T(8,128)(2,1)S(1)}, bf16[384,320]{0,1:T(8,128)(2,1)S(1)}, u32[]{:S(2)}, u32[]{:S(2)}) collective-permute-start(bf16[384,320]{0,1:T(8,128)(2,1)S(1)} %collective-permute-done.2), channel_id=1, source_target_pairs={{0,1},{1,2},{2,3},{3,4},{4,5},{5,6},{6,7},{7,0},{8,9},{9,10},{10,1... | collective-permute-start | bytes 737288 | tf_op jit(solution)/shard_map/ppermute | solution.py:16
  58.4 7.9 %collective-permute-start.4 = (bf16[384,320]{0,1:T(8,128)(2,1)S(1)}, bf16[384,320]{0,1:T(8,128)(2,1)S(1)}, u32[]{:S(2)}, u32[]{:S(2)}) collective-permute-start(bf16[384,320]{0,1:T(8,128)(2,1)S(1)} %collective-permute-done.3), channel_id=1, source_target_pairs={{0,1},{1,2},{2,3},{3,4},{4,5},{5,6},{6,7},{7,0},{8,9},{9,10},{10,1... | collective-permute-start | bytes 737288 | tf_op jit(solution)/shard_map/ppermute | solution.py:16
  66.4 6.5 %collective-permute-start.5 = (bf16[384,320]{0,1:T(8,128)(2,1)S(1)}, bf16[384,320]{0,1:T(8,128)(2,1)S(1)}, u32[]{:S(2)}, u32[]{:S(2)}) collective-permute-start(bf16[384,320]{0,1:T(8,128)(2,1)S(1)} %collective-permute-done.4), channel_id=1, source_target_pairs={{0,1},{1,2},{2,3},{3,4},{4,5},{5,6},{6,7},{7,0},{8,9},{9,10},{10,1... | collective-permute-start | bytes 737288 | tf_op jit(solution)/shard_map/ppermute | solution.py:16
  72.9 6.5 %collective-permute-start.6 = (bf16[384,320]{0,1:T(8,128)(2,1)S(1)}, bf16[384,320]{0,1:T(8,128)(2,1)S(1)}, u32[]{:S(2)}, u32[]{:S(2)}) collective-permute-start(bf16[384,320]{0,1:T(8,128)(2,1)S(1)} %collective-permute-done.5), channel_id=1, source_target_pairs={{0,1},{1,2},{2,3},{3,4},{4,5},{5,6},{6,7},{7,0},{8,9},{9,10},{10,1... | collective-permute-start | bytes 737288 | tf_op jit(solution)/shard_map/ppermute | solution.py:16
  91.7 9.4 %copy-start.4 = (bf16[3072,320]{0,1:T(8,128)(2,1)S(1)}, bf16[3072,320]{0,1:T(8,128)(2,1)}, u32[]{:S(2)}) copy-start(bf16[3072,320]{0,1:T(8,128)(2,1)} %all-gather.2.cloned.1.call-done) | copy-start | bytes 5898244
  108.5 12.4 %copy-start.5 = (f32[320,2048]{1,0:T(8,128)}, f32[320,2048]{1,0:T(8,128)S(1)}, u32[]{:S(2)}) copy-start(f32[320,2048]{1,0:T(8,128)S(1)} %fusion.6) | copy-start | bytes 7864324
  149.3 50.5 %copy-start.1 = (bf16[384,128]{1,0:T(8,128)(2,1)S(1)}, bf16[384,128]{1,0:T(8,128)(2,1)}, u32[]{:S(2)}) copy-start(bf16[384,128]{1,0:T(8,128)(2,1)} %param.8) | copy-start | bytes 294916
  182.3 15.6 %copy-start.3 = (f32[128,2]{0,1:T(2,128)S(1)}, f32[128,2]{0,1:T(2,128)}, u32[]{:S(2)}) copy-start(f32[128,2]{0,1:T(2,128)} %param.10) | copy-start | bytes 3076
Sparse Core Ops, SparseCore 0:
  36.2 30.0 all-gather.1
